TPU v7x, 32 devices: a whole 2x2x4 slice. The times are simulated.
32 devices in a mesh: dp: 16 (over z, y, x), mp: 2 (over core).
Axes of the slice: x: 2, y: 2, z: 4, core: 2. Of those that a mesh axis runs over, the one named last changes fastest.
Arguments:
- short_input: bfloat16 [64, 128, 768], P('dp'), may hold values from -6 to 6
- long_input: bfloat16 [16, 512, 768], P('dp'), may hold values from -6 to 6
- query_weight: bfloat16 [768, 768], P(None, 'mp'), may hold values from -0.21875 to 0.21875
- query_bias: bfloat16 [768], P('mp'), may hold values from -3 to 3
- key_weight: bfloat16 [768, 768], P(None, 'mp'), may hold values from -0.21875 to 0.21875
- value_weight: bfloat16 [768, 768], P(None, 'mp'), may hold values from -0.21875 to 0.21875
- value_bias: bfloat16 [768], P('mp'), may hold values from -3 to 3
- output_weight: bfloat16 [768, 768], P('mp'), may hold values from -0.875 to 0.875
- output_bias: bfloat16 [768], replicated, may hold values from -3 to 3
- gain_one: bfloat16 [768], replicated, may hold values from 0.25 to 1.75
- shift_one: bfloat16 [768], replicated, may hold values from -2 to 2
- upward_weight: bfloat16 [768, 3072], P(None, 'mp'), may hold values from -0.21875 to 0.21875
- upward_bias: bfloat16 [3072], P('mp'), may hold values from -3 to 3
- downward_weight: bfloat16 [3072, 768], P('mp'), may hold values from -0.109375 to 0.109375
- downward_bias: bfloat16 [768], replicated, may hold values from -3 to 3
- gain_two: bfloat16 [768], replicated, may hold values from 0.25 to 1.75
- shift_two: bfloat16 [768], replicated, may hold values from -2 to 2
- short_upstream: bfloat16 [64, 128, 768], P('dp'), may hold values from -6 to 6
- long_upstream: bfloat16 [16, 512, 768], P('dp'), may hold values from -6 to 6
- short_lengths: int32 [64], P('dp'), may hold values from 64 to 128, as said below
- long_lengths: int32 [16], P('dp'), may hold values from 256 to 512, as said below
- live_counts: int32 [16, 2], P('dp'), may hold values from 0 to 4, as said below
Outputs:
- short_output: bfloat16 [64, 128, 768], P('dp')
- long_output: bfloat16 [16, 512, 768], P('dp')
- short_inputgrad: bfloat16 [64, 128, 768], P('dp')
- long_inputgrad: bfloat16 [16, 512, 768], P('dp')
- query_grad: float32 [768, 768], P('dp', 'mp')
- querybias_grad: float32 [768], P(('mp', 'dp'))
- key_grad: float32 [768, 768], P('dp', 'mp')
- value_grad: float32 [768, 768], P('dp', 'mp')
- valuebias_grad: float32 [768], P(('mp', 'dp'))
- output_grad: float32 [768, 768], P('mp', 'dp')
- outbias_grad: float32 [768], P('dp')
- gainone_grad: float32 [768], P('dp')
- shiftone_grad: float32 [768], P('dp')
- upward_grad: float32 [768, 3072], P('dp', 'mp')
- upbias_grad: float32 [3072], P(('mp', 'dp'))
- downward_grad: float32 [3072, 768], P('mp', 'dp')
- downbias_grad: float32 [768], P('dp')
- gaintwo_grad: float32 [768], P('dp')
- shifttwo_grad: float32 [768], P('dp')
Inputs may be any that keep to these rules, and one draw needn't show every extreme that they name: `short_lengths`: in every draw some short slot holds 128 tokens and some holds 64. `long_lengths`: in every draw some long slot holds 512 tokens and some holds 256. `live_counts`: column 0 counts a device's live short slots, 2 to 4; column 1 its live long slots, 0 or 1; the live slots are a device's first ones; in every draw some device has all slots live and another has the fewest of both kinds.
All inputs are finite; a program needn't handle non-finite values.
Results may differ from a plain program's by a relative error of at most 0.02.
Values may be sent and summed in bfloat16 or wider, within the bound.
A program may use at most 128 MiB of HBM per device.

v0:
```python
import functools

import jax
import jax.numpy as jnp
from jax import lax
from jax.experimental import pallas as pl
from jax.experimental.pallas import tpu as pltpu
from jax.sharding import PartitionSpec as P

HEAD = 64
PAIR = 2 * HEAD
NEGATIVE = -1e30
EPSILON = 1e-12
BF = jnp.bfloat16
F32 = jnp.float32
MESH = pl.DeviceIdType.MESH

BITS = 4
X, Y, NEAR, FAR = 0, 1, 2, 3
ORDERS = (
    (X, Y, NEAR, FAR),
    (X, Y, FAR, NEAR),
    (X, NEAR, Y, FAR),
    (X, NEAR, FAR, Y),
    (X, FAR, Y, NEAR),
    (X, FAR, NEAR, Y),
    (Y, X, NEAR, FAR),
    (Y, X, FAR, NEAR),
    (Y, NEAR, X, FAR),
    (Y, NEAR, FAR, X),
    (Y, FAR, X, NEAR),
    (Y, FAR, NEAR, X),
    (NEAR, X, Y, FAR),
    (NEAR, X, FAR, Y),
    (NEAR, Y, X, FAR),
    (NEAR, Y, FAR, X),
    (NEAR, FAR, X, Y),
    (NEAR, FAR, Y, X),
)
PARTS_AT = (0, 8, 12, 14)


def mm(left, right):
    return jnp.dot(left, right, preferred_element_type=F32)


def mm_nt(left, right):
    return lax.dot_general(left, right, (((1,), (1,)), ((), ())), preferred_element_type=F32)


def mm_tn(left, right):
    return lax.dot_general(left, right, (((0,), (0,)), ((), ())), preferred_element_type=F32)


def rows_of(start, size):
    return pl.ds(pl.multiple_of(start, size), size)


def fold(values):
    rows, width = values.shape
    return jnp.sum(values.reshape(rows // 8, 8, width), axis=0)


def place(order, block):
    spot = 0
    for bit in order:
        spot = spot * 2 + ((block >> bit) & 1)
    return spot


class Refs:
    pass


def layer(reduce_here, names, *refs):
    r = Refs()
    for name, ref in zip(names, refs, strict=True):
        setattr(r, name, ref)
    dp, mp = lax.axis_index("dp"), lax.axis_index("mp")
    peer = (dp, 1 - mp)
    half = r.own.shape[1]
    seg_rows = 2 * half
    width = r.x.shape[1]
    local = r.ctx.shape[1]
    pairs = local // PAIR
    heads = local // HEAD
    hidden = r.f.shape[1]
    short_slots, short_length = r.xs.shape[0], r.xs.shape[1]
    long_length = r.xl.shape[1]
    block = r.G0.shape[1]
    tile = 64

    my_bit = [lax.rem(lax.div(dp, 1 << k), 2) for k in range(BITS)]
    across = [(dp + (1 - 2 * my_bit[k]) * (1 << k), mp) for k in range(BITS)]

    loads = {}

    def load(name, src, dst):
        cp = pltpu.make_async_copy(src, dst, r.load_sem.at[len(loads)])
        cp.start()
        loads[name] = cp

    load("xl", r.xl.at[0], r.x.at[pl.ds(seg_rows, seg_rows)])
    for j, source in enumerate((r.wq_h, r.wk_h, r.wv_h)):
        load(f"w{j}", source, r.wqkv.at[:, pl.ds(j * local, local)])

    def load_rest():
        for s in range(short_slots):
            load(f"xs{s}", r.xs.at[s], r.x.at[pl.ds(s * short_length, short_length)])
        load("wo", r.wo_h, r.wo)
        load("wu", r.wu_h, r.wu)
        load("wd", r.wd_h, r.wd)
        load("us", r.us.at[pl.ds(mp * (short_slots // 2), short_slots // 2)], r.ups)
        load("ul", r.ul.at[0, rows_of(mp * half, half)], r.upl)

    barrier = pltpu.get_barrier_semaphore()
    partners = [peer] + (across if reduce_here else [])
    for other in partners:
        pl.semaphore_signal(barrier, inc=1, device_id=other, device_id_type=MESH)

    sends = []

    def remote(src, dst, index, device):
        cp = pltpu.make_async_remote_copy(
            src_ref=src,
            dst_ref=dst,
            send_sem=r.ex_send.at[index],
            recv_sem=r.ex_recv.at[index],
            device_id=device,
            device_id_type=MESH,
        )
        cp.start()
        sends.append(cp)
        return cp

    live_short, live_long = r.live[0, 0], r.live[0, 1]
    long_len = jnp.where(live_long > 0, r.ll[0], 0)

    def short_len(slot):
        return jnp.where(slot < live_short, r.sl[slot], 0)

    def param(ref):
        return ref[...].astype(F32).reshape(1, -1)

    qb, vb, ob, g1, b1 = (param(n) for n in (r.qb, r.vb, r.ob, r.g1, r.b1))
    ub, db, g2, b2 = (param(n) for n in (r.ub, r.db, r.g2, r.b2))

    low_lane = lax.broadcasted_iota(jnp.int32, (1, PAIR), 1) < HEAD

    def first(values):
        return jnp.where(low_lane, values, jnp.zeros_like(values))

    def second(values):
        return jnp.where(low_lane, jnp.zeros_like(values), values)

    def own_start(seg):
        return seg * seg_rows + mp * half

    def peer_start(seg):
        return seg * seg_rows + (1 - mp) * half

    r.acc[...] = jnp.zeros_like(r.acc)
    r.acc_up[...] = jnp.zeros_like(r.acc_up)
    r.acc_qv[...] = jnp.zeros_like(r.acc_qv)

    def project(seg):
        rows = slice(seg * seg_rows, (seg + 1) * seg_rows)
        product = mm(r.x[rows, :], r.wqkv[...])
        r.qkv[rows, :local] = (product[:, :local] + qb).astype(BF) * BF(HEAD**-0.5)
        r.qkv[rows, local : 2 * local] = product[:, local : 2 * local].astype(BF)
        r.qkv[rows, 2 * local :] = (product[:, 2 * local :] + vb).astype(BF)

    def softmax(scores):
        highest = [jnp.max(s, axis=-1, keepdims=True) for s in scores]
        expo = [jnp.exp(s - m) for s, m in zip(scores, highest)]
        total = [1.0 / jnp.sum(e, axis=-1, keepdims=True) for e in expo]
        return [(e * t).astype(BF) for e, t in zip(expo, total)]

    def lanes_of(pair, part=0):
        if isinstance(pair, int):
            return slice(part * local + pair * PAIR, part * local + (pair + 1) * PAIR)
        return rows_of(part * local + pair * PAIR, PAIR)

    def parts_of(ref, rows, pair):
        return [ref[rows, lanes_of(pair, part)] for part in range(3)]

    def slot_rows(s):
        return slice(s * short_length, (s + 1) * short_length)

    long_rows = slice(seg_rows, 2 * seg_rows)

    def attend_long():
        position = lax.broadcasted_iota(jnp.int32, (1, long_length), 1)
        bias = jnp.where(position < long_len, 0.0, NEGATIVE)
        for pair in range(pairs):
            qp, kp, vp = parts_of(r.qkv, long_rows, pair)
            parts = []
            for j, pick in enumerate((first, second)):
                (probs,) = softmax([mm_nt(pick(qp), kp) + bias])
                r.pl[2 * pair + j] = probs
                parts.append(mm(probs, vp))
            r.ctx[long_rows, lanes_of(pair)] = jnp.where(low_lane, *parts).astype(BF)

    def attend_short():
        position = lax.broadcasted_iota(jnp.int32, (1, short_length), 1)
        scores = []
        for s in range(short_slots):
            bias = jnp.where(position < short_len(s), 0.0, NEGATIVE)
            for pair in range(pairs):
                qp, kp, _ = parts_of(r.qkv, slot_rows(s), pair)
                scores += [mm_nt(first(qp), kp) + bias, mm_nt(second(qp), kp) + bias]
        probs = softmax(scores)
        for s in range(short_slots):
            for pair in range(pairs):
                parts = []
                for head in (2 * pair, 2 * pair + 1):
                    r.ps[s, head] = probs[s * heads + head]
                    parts.append(mm(probs[s * heads + head], r.qkv[slot_rows(s), lanes_of(pair, 2)]))
                r.ctx[slot_rows(s), lanes_of(pair)] = jnp.where(low_lane, *parts).astype(BF)

    def exchange(stage, seg, left, right, product, between=lambda: None):
        index = 2 * stage + seg
        r.out_buf[index] = product(left[rows_of(peer_start(seg), half), :], right[...]).astype(BF)
        cp = remote(r.out_buf.at[index], r.in_buf.at[index], index, peer)
        between()
        r.own[seg] = product(left[rows_of(own_start(seg), half), :], right[...])
        return cp

    def share(index, seg, ref):
        rows = rows_of(own_start(seg), half)
        return remote(ref.at[rows], ref.at[rows], index, peer)

    def norm(values):
        mean = jnp.mean(values, axis=-1, keepdims=True)
        centred = values - mean
        scale = lax.rsqrt(jnp.mean(centred * centred, axis=-1, keepdims=True) + EPSILON)
        return centred * scale, scale

    def norm_back(normed, scale, grad):
        return scale * (
            grad
            - jnp.mean(grad, axis=-1, keepdims=True)
            - normed * jnp.mean(grad * normed, axis=-1, keepdims=True)
        )

    def norm_one(seg):
        for t in range(half // tile):
            mine = slice(seg * half + t * tile, seg * half + (t + 1) * tile)
            here = slice(t * tile, (t + 1) * tile)
            rows = rows_of(own_start(seg) + t * tile, tile)
            total = r.own[seg, here, :] + r.in_buf[seg, here, :].astype(F32) + ob
            normed, scale = norm(r.x[rows, :].astype(F32) + total)
            r.n1[mine, :] = normed
            r.r1[mine, :] = scale
            r.h[rows, :] = (normed * g1 + b1).astype(BF)

    def up(seg):
        rows = slice(seg * seg_rows, (seg + 1) * seg_rows)
        step = 256
        for j in range(hidden // step):
            cols = slice(j * step, (j + 1) * step)
            pre = mm(r.h[rows, :], r.wu[:, cols]) + ub[:, cols]
            phi = 0.5 + 0.5 * lax.erf(pre * (0.5**0.5))
            r.f[rows, cols] = (pre * phi).astype(BF)
            r.gp[rows, cols] = (phi + pre * (jnp.exp(pre * pre * -0.5) * 0.3989422804014327)).astype(BF)

    def norm_two(seg):
        for t in range(half // tile):
            mine = slice(seg * half + t * tile, seg * half + (t + 1) * tile)
            here = slice(t * tile, (t + 1) * tile)
            rows = rows_of(own_start(seg) + t * tile, tile)
            row = lax.broadcasted_iota(jnp.int32, (tile, 1), 0)
            if seg == 0:
                slot, inner = t * tile // short_length, t * tile % short_length
                keep = row + inner < short_len(mp * (short_slots // 2) + slot)
                upstream = r.ups[slot, inner : inner + tile, :]
            else:
                keep = row + (mp * half + t * tile) < long_len
                upstream = r.upl[here, :]
            keep = keep.astype(F32)
            hidden_state = r.n1[mine, :] * g1 + b1
            total = r.own[seg, here, :] + r.in_buf[2 + seg, here, :].astype(F32) + db
            normed, scale = norm(hidden_state + total)
            r.out[seg, here, :] = (keep * (normed * g2 + b2)).astype(BF)
            grad = keep * upstream.astype(F32)
            r.acc[0] += fold(grad * normed)
            r.acc[1] += fold(grad)
            dsecond = norm_back(normed, scale, grad * g2)
            low = dsecond.astype(BF)
            r.acc[2] += fold(low.astype(F32))
            r.ds[mine, :] = dsecond
            r.do[rows, :] = low

    def norm_one_back(seg):
        for t in range(half // tile):
            mine = slice(seg * half + t * tile, seg * half + (t + 1) * tile)
            here = slice(t * tile, (t + 1) * tile)
            rows = rows_of(own_start(seg) + t * tile, tile)
            grad = r.ds[mine, :] + r.own[seg, here, :] + r.in_buf[4 + seg, here, :].astype(F32)
            normed = r.n1[mine, :]
            r.acc[3] += fold(grad * normed)
            r.acc[4] += fold(grad)
            dfirst = norm_back(normed, r.r1[mine, :], grad * g1)
            low = dfirst.astype(BF)
            r.acc[5] += fold(low.astype(F32))
            r.ds[mine, :] = dfirst
            r.da[rows, :] = low

    def active_back(seg):
        for part in range(2):
            rows = slice(seg * seg_rows + part * half, seg * seg_rows + (part + 1) * half)
            step = 512
            for j in range(hidden // step):
                yield
                cols = slice(j * step, (j + 1) * step)
                low = (mm_nt(r.do[rows, :], r.wd[cols, :]) * r.gp[rows, cols].astype(F32)).astype(BF)
                r.acc_up[:, cols] += fold(low.astype(F32))
                r.gp[rows, cols] = low

    def dscores(rows, pair, probs):
        vp, dc = r.qkv[rows, lanes_of(pair, 2)], r.dctx[rows, lanes_of(pair)]
        product = dc.astype(F32) * r.ctx[rows, lanes_of(pair)].astype(F32)
        held = []
        for j, pick in enumerate((first, second)):
            inner = jnp.sum(pick(product), axis=-1, keepdims=True)
            held.append((probs[j].astype(F32) * (mm_nt(pick(dc), vp) - inner)).astype(BF))
        return held

    def heads_back(rows, pair, probs, held):
        qp, kp, _ = parts_of(r.qkv, rows, pair)
        dc = r.dctx[rows, lanes_of(pair)]
        dq = jnp.where(low_lane, mm(held[0], kp), mm(held[1], kp)) * HEAD**-0.5
        r.dqkv[rows, lanes_of(pair)] = dq.astype(BF)
        r.dqkv[rows, lanes_of(pair, 1)] = jnp.where(low_lane, mm_tn(held[0], qp), mm_tn(held[1], qp)).astype(BF)
        r.dqkv[rows, lanes_of(pair, 2)] = jnp.where(low_lane, mm_tn(probs[0], dc), mm_tn(probs[1], dc)).astype(BF)

    def attend_long_back(pair):
        probs = [r.pl[2 * pair], r.pl[2 * pair + 1]]
        heads_back(long_rows, pair, probs, dscores(long_rows, pair, probs))

    def attend_short_back():
        each = [(s, pair) for s in range(short_slots) for pair in range(pairs)]
        probs = [[r.ps[s, 2 * pair], r.ps[s, 2 * pair + 1]] for s, pair in each]
        held = [dscores(slot_rows(s), pair, p) for (s, pair), p in zip(each, probs)]
        for (s, pair), p, h in zip(each, probs, held):
            heads_back(slot_rows(s), pair, p, h)

    begin, flight = {}, {}

    def half_copy(c, p):
        n = 8 >> p
        bit = ORDERS[KINDS[c]][p]
        start = begin.get(c, 0)
        held, landed = getattr(r, f"G{c}"), getattr(r, f"R{c}")
        cp = pltpu.make_async_remote_copy(
            src_ref=held.at[pl.ds(start + (1 - my_bit[bit]) * n, n)],
            dst_ref=landed.at[pl.ds(PARTS_AT[p], n)],
            send_sem=r.rs_send.at[c, p],
            recv_sem=r.rs_recv.at[c, p],
            device_id=across[bit],
            device_id_type=MESH,
        )
        cp.start()
        sends.append(cp)
        begin[c] = start + my_bit[bit] * n
        flight[c] = (p, cp)

    def operands(start, stop):
        for left, right in ((r.do, r.f), (r.h, r.gp), (r.da, r.ctx), (r.x, r.dqkv)):
            span = right.shape[1]
            if start < span:
                return left, right, slice(start, stop)
            start, stop = start - span, stop - span

    def gradient(begins, ends):
        blocks = 1 << BITS
        part = width // 2
        base = COLUMNS[begins]
        left, right, cols = operands(base, COLUMNS[ends])
        orders = [ORDERS[KINDS[c]] if reduce_here else (3, 2, 1, 0) for c in range(begins, ends)]

        @pl.loop(0, 2)
        def _(m):
            piece = mm_tn(left[:, rows_of(m * part, part)], right[:, cols]).astype(BF)
            for c, order in zip(range(begins, ends), orders):
                held = getattr(r, f"G{c}")
                own = piece[:, COLUMNS[c] - base : COLUMNS[c + 1] - base]
                for b in range(blocks // 2):
                    held[place(order, b) + m * place(order, blocks // 2)] = own[b * block : (b + 1) * block]

        if reduce_here:
            for c in range(begins, ends):
                half_copy(c, 0)

    vector = [None, 0]

    def vector_copy(k):
        r.vec_out[k] = r.vec[...].astype(BF)
        device = peer if k == 0 else across[k - 1]
        vector[:] = remote(r.vec_out.at[k], r.vec_in.at[k], 22 + k, device), k

    def vector_advance():
        cp, k = vector
        cp.wait_recv()
        rows = slice(8 if k == 0 else 0, 16)
        r.vec[rows, :] = (r.vec_out[k].astype(F32) + r.vec_in[k].astype(F32))[rows]
        if k < BITS and reduce_here:
            vector_copy(k + 1)

    def advance(c):
        p, cp = flight.pop(c)
        n = 8 >> p
        held, landed = getattr(r, f"G{c}"), getattr(r, f"R{c}")
        cp.wait_recv()
        if p < BITS - 1:
            mine = pl.ds(begin[c], n)
            held[mine] = held[mine] + landed[PARTS_AT[p] : PARTS_AT[p] + n]
            half_copy(c, p + 1)
        else:
            total = held[begin[c]].astype(F32) + landed[PARTS_AT[p]].astype(F32)
            cols = slice(COLUMNS[c], COLUMNS[c + 1])
            r.held_rows[:, cols] = total
            cp = pltpu.make_async_copy(r.held_rows.at[:, cols], r.rows.at[:, cols], r.row_sem.at[c])
            cp.start()
            outs.append(cp)

    todo = list(EVENTS) if reduce_here else []
    marks = list(MARKS)

    def handle():
        c = todo.pop(0)
        if c < CHUNKS:
            advance(c)
        else:
            vector_advance()

    def point():
        upto = marks.pop(0) if marks else len(EVENTS)
        while todo and len(EVENTS) - len(todo) < upto:
            handle()

    def gradients(group):
        for job, begins, ends in JOBS:
            if job == group:
                point()
                gradient(begins, ends)

    for name in ("xl", "w0", "w1", "w2"):
        loads[name].wait()
    load_rest()
    project(1)
    attend_long()
    loads["wo"].wait()
    pl.semaphore_wait(barrier, len(partners))
    ex = {}
    ex["a1"] = exchange(0, 1, r.ctx, r.wo, mm)
    for s in range(short_slots):
        loads[f"xs{s}"].wait()
    project(0)
    ex["a1"].wait_recv()
    norm_one(1)
    ex["h1"] = share(8, 1, r.h)
    attend_short()
    ex["a0"] = exchange(0, 0, r.ctx, r.wo, mm)
    loads["wu"].wait()
    loads["wd"].wait()
    ex["h1"].wait_recv()
    up(1)
    ex["a0"].wait_recv()
    norm_one(0)
    ex["h0"] = share(9, 0, r.h)
    ex["o1"] = exchange(1, 1, r.f, r.wd, mm)
    ex["h0"].wait_recv()
    up(0)
    ex["o0"] = exchange(1, 0, r.f, r.wd, mm)
    loads["us"].wait()
    loads["ul"].wait()
    outs, arrivals = [], []

    def publish(index, seg, short_ref, long_ref, held):
        if seg == 0:
            for s in range(short_slots // 2):
                piece = held.at[0, pl.ds(s * short_length, short_length)]
                target = short_ref.at[mp * (short_slots // 2) + s]
                cp = pltpu.make_async_copy(piece, target, r.out_sem.at[index + s])
                cp.start()
                outs.append(cp)
                arrivals.append(remote(piece, target, 16 + index + s, peer))
        else:
            target = long_ref.at[0, rows_of(mp * half, half)]
            cp = pltpu.make_async_copy(held.at[1], target, r.out_sem.at[index + 2])
            cp.start()
            outs.append(cp)
            arrivals.append(remote(held.at[1], target, 16 + index + 2, peer))

    for seg in (1, 0):
        ex[f"o{seg}"].wait_recv()
        norm_two(seg)
        ex[f"do{seg}"] = share(10 + seg, seg, r.do)
    ex["do1"].wait_recv()

    early, late = active_back(1), active_back(0)
    for _ in range(EARLY):
        next(early)
    ex["do0"].wait_recv()
    gradients("d")
    point()
    publish(0, 1, r.os, r.ol, r.out)
    publish(0, 0, r.os, r.ol, r.out)
    for pieces in (early, late):
        for _ in pieces:
            point()
    gradients("u")
    for seg in (1, 0):
        point()
        ex[f"dh{seg}"] = exchange(2, seg, r.gp, r.wu, mm_nt, point)
    for seg in (1, 0):
        point()
        ex[f"dh{seg}"].wait_recv()
        norm_one_back(seg)
        ex[f"da{seg}"] = share(12 + seg, seg, r.da)
    for seg in (1, 0):
        point()
        ex[f"da{seg}"].wait_recv()
        rows = slice(seg * seg_rows, (seg + 1) * seg_rows)
        r.dctx[rows, :] = mm_nt(r.da[rows, :], r.wo[...]).astype(BF)
    gradients("o")
    point()
    pl.loop(0, pairs)(attend_long_back)
    point()
    attend_short_back()
    gradients("q")
    point()
    for j in range(2):
        r.acc_qv[:, j * local : (j + 1) * local] = fold(r.dqkv[:, 2 * j * local : (2 * j + 1) * local].astype(F32))

    def total_of(values):
        return jnp.sum(values, axis=0, keepdims=True)

    r.vec[...] = jnp.zeros_like(r.vec)
    r.vec[0:1, :] = total_of(r.acc_qv[...])
    r.vec[1:2, :] = total_of(r.acc_up[:, :width])
    r.vec[2:3, :] = total_of(r.acc_up[:, width:])
    for j in range(6):
        r.vec[8 + j : 9 + j, :] = total_of(r.acc[j])
    vector_copy(0)

    def input_part(rows):
        return mm_nt(r.dqkv[rows, :], r.wqkv[...])

    for seg in (1, 0):
        index = 6 + seg
        point()
        r.out_buf[index] = input_part(rows_of(peer_start(seg), half)).astype(BF)
        ex[f"dx{seg}"] = remote(r.out_buf.at[index], r.in_buf.at[index], index, peer)
        point()
        r.own[seg] = input_part(rows_of(own_start(seg), half))
    for seg in (1, 0):
        point()
        ex[f"dx{seg}"].wait_recv()
        dfirst = r.ds[seg * half : (seg + 1) * half, :]
        r.dxo[seg] = (dfirst + r.own[seg] + r.in_buf[6 + seg].astype(F32)).astype(BF)
        publish(3, seg, r.dxs, r.dxl, r.dxo)
    if reduce_here:
        while todo:
            handle()
    else:
        for c in range(CHUNKS):
            cp = pltpu.make_async_copy(
                getattr(r, f"G{c}"), r.grads.at[:, :, pl.ds(COLUMNS[c], COLUMNS[c + 1] - COLUMNS[c])], r.out_sem.at[6]
            )
            cp.start()
            cp.wait()
        vector_advance()
    r.sums[...] = r.vec[...]

    for cp in outs:
        cp.wait()
    for cp in arrivals:
        cp.wait_recv()
    for cp in sends:
        cp.wait_send()


COLUMNS = (
    0, 256, 512, 768, 1024, 1280, 1536, 1792, 2048, 2304, 2560, 2816, 3072, 3200, 3328, 3456, 3584, 3712, 3840,
    3968, 4096, 4224, 4352, 4480, 4608,
)
KINDS = (
    11, 13, 3, 11, 3, 14, 7, 7, 7, 4, 8, 7, 0, 3, 14, 8, 6, 3, 8, 6, 6, 0, 2, 0,
)
CHUNKS = len(KINDS)
JOBS = (
    ("d", 0, 1),
    ("d", 1, 2),
    ("d", 2, 4),
    ("d", 4, 6),
    ("u", 6, 8),
    ("u", 8, 10),
    ("u", 10, 12),
    ("o", 12, 15),
    ("q", 15, 24),
)
EVENTS = (
    0, 2, 3, 1, 4, 6, 9, 7, 2, 0, 8, 1, 4, 13, 10, 3, 6, 17, 7, 15, 8, 24, 11, 22, 13, 18, 16, 17, 10, 6, 24, 7,
    19, 5, 11, 15, 16, 18, 8, 20, 12, 10, 24, 0, 14, 19, 3, 15, 21, 5, 16, 18, 11, 23, 20, 24, 9, 14, 12, 19,
    22, 21, 2, 5, 1, 23, 4, 20, 14, 13, 17, 9, 12, 22, 21, 23, 6, 7, 8, 0, 10, 3, 15, 16, 11, 18, 24, 19, 2, 1,
    5, 4, 13, 20, 17, 9, 14, 12, 22, 21, 23,
)
MARKS = (
    0, 0, 0, 0, 0, 0, 0, 0, 0, 0, 0, 0, 0, 0, 1, 1, 1, 2, 2, 3, 4, 5, 5, 7, 7, 10, 13, 14, 14, 15, 15, 16, 17,
    17,
)
EARLY = 5


def shards(n_dp, *args):
    (
        xs, xl, wq, qb, wk, wv, vb, wo, ob, g1, b1, wu, ub, wd, db, g2, b2, us, ul, sl, ll, live,
    ) = args
    short_slots, short_length, width = xs.shape
    long_length = xl.shape[1]
    local, hidden = wq.shape[1], wu.shape[1]
    heads = local // HEAD
    rows = short_slots * short_length + xl.shape[0] * long_length
    half = long_length // 2
    reduce_here = n_dp == 1 << BITS
    blocks = 1 << BITS
    block = width // blocks
    columns = 4 * local + 2 * hidden
    spans = [COLUMNS[c + 1] - COLUMNS[c] for c in range(CHUNKS)]
    assert COLUMNS[-1] == columns
    any_spec = pl.BlockSpec(memory_space=pl.ANY)
    vmem = pl.BlockSpec(memory_space=pltpu.VMEM)
    smem = pl.BlockSpec(memory_space=pltpu.SMEM)
    inputs = [
        ("sl", sl, smem), ("ll", ll, smem), ("live", live, smem),
        ("xs", xs, any_spec), ("xl", xl, any_spec), ("us", us, any_spec), ("ul", ul, any_spec),
        ("wq_h", wq, any_spec), ("wk_h", wk, any_spec), ("wv_h", wv, any_spec), ("wo_h", wo, any_spec),
        ("wu_h", wu, any_spec), ("wd_h", wd, any_spec),
        ("qb", qb, vmem), ("vb", vb, vmem), ("ob", ob, vmem), ("g1", g1, vmem), ("b1", b1, vmem),
        ("ub", ub, vmem), ("db", db, vmem), ("g2", g2, vmem), ("b2", b2, vmem),
    ]
    sds = jax.ShapeDtypeStruct
    outputs = [
        ("os", sds(xs.shape, BF), any_spec), ("ol", sds(xl.shape, BF), any_spec),
        ("dxs", sds(xs.shape, BF), any_spec), ("dxl", sds(xl.shape, BF), any_spec),
    ]
    if reduce_here:
        outputs.append(("rows", sds((block, columns), F32), any_spec))
    else:
        outputs.append(("grads", sds((blocks, block, columns), BF), any_spec))
    outputs.append(("sums", sds((16, width), F32), vmem))
    v = pltpu.VMEM
    dma = pltpu.SemaphoreType.DMA
    scratch = [
        ("x", v((rows, width), BF)), ("ups", v((short_slots // 2, short_length, width), BF)), ("upl", v((half, width), BF)),
        ("wqkv", v((width, 3 * local), BF)), ("wo", v(wo.shape, BF)),
        ("wu", v(wu.shape, BF)), ("wd", v(wd.shape, BF)),
        ("qkv", v((rows, 3 * local), BF)),
        ("pl", v((heads, long_length, long_length), BF)), ("ps", v((short_slots, heads, short_length, short_length), BF)),
        ("ctx", v((rows, local), BF)), ("n1", v((2 * half, width), F32)), ("r1", v((2 * half, 1), F32)),
        ("h", v((rows, width), BF)), ("f", v((rows, hidden), BF)), ("gp", v((rows, hidden), BF)),
        ("do", v((rows, width), BF)), ("ds", v((2 * half, width), F32)), ("da", v((rows, width), BF)),
        ("dctx", v((rows, local), BF)), ("dqkv", v((rows, 3 * local), BF)),
        ("own", v((2, half, width), F32)), ("out_buf", v((8, half, width), BF)), ("in_buf", v((8, half, width), BF)),
        ("out", v((2, half, width), BF)), ("dxo", v((2, half, width), BF)),
        ("acc", v((6, 8, width), F32)), ("acc_up", v((8, hidden), F32)), ("acc_qv", v((8, 2 * local), F32)),
        ("vec", v((16, width), F32)), ("vec_out", v((5, 16, width), BF)), ("vec_in", v((5, 16, width), BF)),
        ("load_sem", dma((16,))), ("out_sem", dma((8,))), ("ex_send", dma((28,))), ("ex_recv", dma((28,))),
        ("held_rows", v((block, columns), F32)), ("row_sem", dma((len(spans),))),
        ("rs_send", dma((len(spans), BITS))), ("rs_recv", dma((len(spans), BITS))),
    ]
    for c, span in enumerate(spans):
        scratch.append((f"G{c}", v((blocks, block, span), BF)))
        scratch.append((f"R{c}", v((blocks - 1 if reduce_here else 1, block, span), BF)))
    names = [n for n, *_ in inputs] + [n for n, *_ in outputs] + [n for n, *_ in scratch]
    macs = rows * width * (8 * local + 6 * hidden)
    results = pl.pallas_call(
        functools.partial(layer, reduce_here, names),
        out_shape=[o[1] for o in outputs],
        in_specs=[i[2] for i in inputs],
        out_specs=[o[2] for o in outputs],
        scratch_shapes=[s[1] for s in scratch],
        cost_estimate=pl.CostEstimate(flops=2 * macs, bytes_accessed=20 << 20, transcendentals=0),
        compiler_params=pltpu.CompilerParams(
            collective_id=0, has_side_effects=True, vmem_limit_bytes=62 << 20
        ),
    )(*[i[1] for i in inputs])
    got = dict(zip([o[0] for o in outputs], results, strict=True))
    if not reduce_here:
        grads = got["grads"].reshape(width, columns).astype(F32)
        got["rows"] = lax.psum_scatter(grads, "dp", scatter_dimension=0, tiled=True)
        got["sums"] = lax.psum(got["sums"], "dp")
    block = width // n_dp
    finals = [
        ("os", sds(xs.shape, BF), any_spec), ("ol", sds(xl.shape, BF), any_spec),
        ("dxs", sds(xs.shape, BF), any_spec), ("dxl", sds(xl.shape, BF), any_spec),
        ("gq", sds((block, local), F32), any_spec), ("g_qb", sds((local // n_dp,), F32), vmem),
        ("gk", sds((block, local), F32), any_spec), ("gv", sds((block, local), F32), any_spec),
        ("g_vb", sds((local // n_dp,), F32), vmem), ("gout", sds((block, local), F32), any_spec),
        ("g_ob", sds((block,), F32), vmem), ("g_gain1", sds((block,), F32), vmem), ("g_shift1", sds((block,), F32), vmem),
        ("gup", sds((block, hidden), F32), any_spec), ("g_ub", sds((hidden // n_dp,), F32), vmem),
        ("gdown", sds((block, hidden), F32), any_spec),
        ("g_db", sds((block,), F32), vmem), ("g_gain2", sds((block,), F32), vmem), ("g_shift2", sds((block,), F32), vmem),
    ]
    sources = ("os", "ol", "dxs", "dxl", "rows", "sums")
    names = ["in_" + n for n in sources] + [f[0] for f in finals] + ["held_" + n for n in sources[:5]] + ["into", "out"]
    results = pl.pallas_call(
        functools.partial(place_results, n_dp, names),
        out_shape=[f[1] for f in finals],
        in_specs=[any_spec] * 5 + [vmem],
        out_specs=[f[2] for f in finals],
        scratch_shapes=[v(got[n].shape, got[n].dtype) for n in sources[:5]] + [dma((10,)), dma((10,))],
        cost_estimate=pl.CostEstimate(flops=0, bytes_accessed=8 << 20, transcendentals=0),
        compiler_params=pltpu.CompilerParams(vmem_limit_bytes=62 << 20),
    )(*[got[n] for n in sources])
    return tuple(result.T if f[0] in ("gout", "gdown") else result for f, result in zip(finals, results, strict=True))


def place_results(n_dp, names, *refs):
    r = Refs()
    for name, ref in zip(names, refs, strict=True):
        setattr(r, name, ref)
    moves = []
    at = 0
    for ref in (r.gdown, r.gup, r.gout, r.gq, r.gk, r.gv):
        cols = slice(at, at + ref.shape[1])
        moves.append((r.in_rows.at[:, cols], r.held_rows.at[:, cols], ref))
        at += ref.shape[1]
    moves += [(getattr(r, "in_" + n), getattr(r, "held_" + n), getattr(r, n)) for n in ("os", "ol", "dxs", "dxl")]
    into = [pltpu.make_async_copy(source, held, r.into.at[j]) for j, (source, held, _) in enumerate(moves)]
    out = [pltpu.make_async_copy(held, target, r.out.at[j]) for j, (_, held, target) in enumerate(moves)]
    for cp in into:
        cp.start()
    for cp, back in zip(into, out):
        cp.wait()
        back.start()
    dp = lax.axis_index("dp")
    local = r.gq.shape[1]
    width = r.in_sums.shape[1]

    def turn(start):
        return pltpu.roll(r.in_sums[...], lax.rem(2 * width - start, width), 1)

    size = r.g_ob.shape[0]
    turned = turn(dp * size)
    for j, ref in enumerate((r.g_gain2, r.g_shift2, r.g_db, r.g_gain1, r.g_shift1, r.g_ob)):
        ref[...] = turned[8 + j : 9 + j, :size].reshape(size)
    size = r.g_qb.shape[0]
    turned = turn(dp * size)
    r.g_qb[...] = turned[0:1, :size].reshape(size)
    r.g_vb[...] = turned[0:1, local : local + size].reshape(size)
    size = r.g_ub.shape[0]
    turned = turn(lax.rem(dp * size, width))
    r.g_ub[...] = jnp.where(dp * size < width, turned[1:2, :size], turned[2:3, :size]).reshape(size)
    for cp in out:
        cp.wait()


def solution(mesh):
    in_specs = (
        P("dp", None, None), P("dp", None, None), P(None, "mp"), P("mp"), P(None, "mp"), P(None, "mp"), P("mp"),
        P("mp", None), P(), P(), P(), P(None, "mp"), P("mp"), P("mp", None), P(), P(), P(),
        P("dp", None, None), P("dp", None, None), P("dp"), P("dp"), P("dp", None),
    )
    out_specs = (
        P("dp", None, None), P("dp", None, None), P("dp", None, None), P("dp", None, None),
        P("dp", "mp"), P(("mp", "dp")), P("dp", "mp"), P("dp", "mp"), P(("mp", "dp")), P("mp", "dp"),
        P("dp"), P("dp"), P("dp"), P("dp", "mp"), P(("mp", "dp")), P("mp", "dp"), P("dp"), P("dp"), P("dp"),
    )
    return jax.shard_map(
        functools.partial(shards, mesh.shape["dp"]),
        mesh=mesh, in_specs=in_specs, out_specs=out_specs, check_vma=False,
    )
```

profile of v0, /device:TPU:0, one launch (start us, length us, event | category | flops | bytes accessed | tf_op | source)
XLA Modules:
  0.0 94.2 jit_solution(1526777850162957160)
XLA Ops:
  1.3 87.6 %shard_map.357 = (bf16[4,128,768]{2,1,0:T(8,128)(2,1)}, bf16[1,512,768]{2,1,0:T(8,128)(2,1)}, bf16[4,128,768]{2,1,0:T(8,128)(2,1)}, bf16[1,512,768]{2,1,0:T(8,12...) custom-call(s32[4]{0:T(128)} %refs_0_.1, s32[1]{0:T(128)S(6)} %copy.41.refs_1_, s32[1,2]{1,0:T(1,128)} %refs_2_.1, ...), custom_call_target="tpu_custom_call" | custom-call | flops 19327352832 | bytes 20971520 | tf_op jit(solution)/shard_map/pallas_call | solution.py:679
  88.9 5.1 %shard_map.358 = (bf16[4,128,768]{2,1,0:T(8,128)(2,1)}, bf16[1,512,768]{2,1,0:T(8,128)(2,1)}, bf16[4,128,768]{2,1,0:T(8,128)(2,1)}, bf16[1,512,768]{2,1,0:T(8,12...) custom-call(bf16[4,128,768]{2,1,0:T(8,128)(2,1)} %get-tuple-element., ...), custom_call_target="tpu_custom_call" | custom-call | bytes 8388608 | tf_op jit(solution)/shard_map/pallas_call | solution.py:709
where the time goes:
time: 94.4 us; the launch traced here: 94.2 us
  Pallas kernels  92.7 us (98%)
  between operations  1.5 us (2%)
    pallas_call x1, Pallas kernels, shards(): pl.pallas_call(functools.partial(layer, reduce_here, names), out_shape=[o...  87.6 us
    pallas_call x1, Pallas kernels, shards(): pl.pallas_call(functools.partial(place_results, n_dp, names), out_shape=[...  5.1 us

commit v1 on v0

--- a/solution.py
+++ b/solution.py
@@ -93,6 +93,11 @@
     my_bit = [lax.rem(lax.div(dp, 1 << k), 2) for k in range(BITS)]
     across = [(dp + (1 - 2 * my_bit[k]) * (1 << k), mp) for k in range(BITS)]
 
+    barrier = pltpu.get_barrier_semaphore()
+    partners = [peer] + (across if reduce_here else [])
+    for other in partners:
+        pl.semaphore_signal(barrier, inc=1, device_id=other, device_id_type=MESH)
+
     loads = {}
 
     def load(name, src, dst):
@@ -112,11 +117,6 @@
         load("wd", r.wd_h, r.wd)
         load("us", r.us.at[pl.ds(mp * (short_slots // 2), short_slots // 2)], r.ups)
         load("ul", r.ul.at[0, rows_of(mp * half, half)], r.upl)
-
-    barrier = pltpu.get_barrier_semaphore()
-    partners = [peer] + (across if reduce_here else [])
-    for other in partners:
-        pl.semaphore_signal(barrier, inc=1, device_id=other, device_id_type=MESH)
 
     sends = []
 
@@ -254,8 +254,8 @@
             r.r1[mine, :] = scale
             r.h[rows, :] = (normed * g1 + b1).astype(BF)
 
-    def up(seg):
-        rows = slice(seg * seg_rows, (seg + 1) * seg_rows)
+    def up(start):
+        rows = rows_of(start, half)
         step = 256
         for j in range(hidden // step):
             cols = slice(j * step, (j + 1) * step)
@@ -311,11 +311,11 @@
             rows = slice(seg * seg_rows + part * half, seg * seg_rows + (part + 1) * half)
             step = 512
             for j in range(hidden // step):
-                yield
                 cols = slice(j * step, (j + 1) * step)
                 low = (mm_nt(r.do[rows, :], r.wd[cols, :]) * r.gp[rows, cols].astype(F32)).astype(BF)
                 r.acc_up[:, cols] += fold(low.astype(F32))
                 r.gp[rows, cols] = low
+                yield
 
     def dscores(rows, pair, probs):
         vp, dc = r.qkv[rows, lanes_of(pair, 2)], r.dctx[rows, lanes_of(pair)]
@@ -406,6 +406,10 @@
         r.vec[rows, :] = (r.vec_out[k].astype(F32) + r.vec_in[k].astype(F32))[rows]
         if k < BITS and reduce_here:
             vector_copy(k + 1)
+        else:
+            cp = pltpu.make_async_copy(r.vec, r.sums, r.out_sem.at[7])
+            cp.start()
+            outs.append(cp)
 
     def advance(c):
         p, cp = flight.pop(c)
@@ -450,28 +454,30 @@
     load_rest()
     project(1)
     attend_long()
+    for s in range(short_slots):
+        loads[f"xs{s}"].wait()
+    project(0)
     loads["wo"].wait()
     pl.semaphore_wait(barrier, len(partners))
     ex = {}
     ex["a1"] = exchange(0, 1, r.ctx, r.wo, mm)
-    for s in range(short_slots):
-        loads[f"xs{s}"].wait()
-    project(0)
+    attend_short()
     ex["a1"].wait_recv()
     norm_one(1)
     ex["h1"] = share(8, 1, r.h)
-    attend_short()
     ex["a0"] = exchange(0, 0, r.ctx, r.wo, mm)
     loads["wu"].wait()
     loads["wd"].wait()
+    up(own_start(1))
     ex["h1"].wait_recv()
-    up(1)
+    up(peer_start(1))
     ex["a0"].wait_recv()
     norm_one(0)
     ex["h0"] = share(9, 0, r.h)
     ex["o1"] = exchange(1, 1, r.f, r.wd, mm)
+    up(own_start(0))
     ex["h0"].wait_recv()
-    up(0)
+    up(peer_start(0))
     ex["o0"] = exchange(1, 0, r.f, r.wd, mm)
     loads["us"].wait()
     loads["ul"].wait()
@@ -572,7 +578,6 @@
             cp.start()
             cp.wait()
         vector_advance()
-    r.sums[...] = r.vec[...]
 
     for cp in outs:
         cp.wait()
@@ -583,35 +588,35 @@
 
 
 COLUMNS = (
-    0, 256, 512, 768, 1024, 1280, 1536, 1792, 2048, 2304, 2560, 2816, 3072, 3200, 3328, 3456, 3584, 3712, 3840,
-    3968, 4096, 4224, 4352, 4480, 4608,
+    0, 128, 256, 384, 512, 768, 1024, 1280, 1536, 1792, 2048, 2304, 2560, 2816, 3072, 3328, 3456, 3712, 3968,
+    4224, 4352, 4480, 4608,
 )
 KINDS = (
-    11, 13, 3, 11, 3, 14, 7, 7, 7, 4, 8, 7, 0, 3, 14, 8, 6, 3, 8, 6, 6, 0, 2, 0,
+    14, 3, 16, 11, 7, 3, 4, 9, 5, 9, 0, 2, 6, 6, 9, 14, 1, 8, 0, 2, 0, 6,
 )
 CHUNKS = len(KINDS)
 JOBS = (
-    ("d", 0, 1),
-    ("d", 1, 2),
+    ("d", 0, 2),
     ("d", 2, 4),
     ("d", 4, 6),
-    ("u", 6, 8),
+    ("d", 6, 8),
     ("u", 8, 10),
     ("u", 10, 12),
-    ("o", 12, 15),
-    ("q", 15, 24),
+    ("u", 12, 14),
+    ("o", 14, 16),
+    ("q", 16, 22),
 )
 EVENTS = (
-    0, 2, 3, 1, 4, 6, 9, 7, 2, 0, 8, 1, 4, 13, 10, 3, 6, 17, 7, 15, 8, 24, 11, 22, 13, 18, 16, 17, 10, 6, 24, 7,
-    19, 5, 11, 15, 16, 18, 8, 20, 12, 10, 24, 0, 14, 19, 3, 15, 21, 5, 16, 18, 11, 23, 20, 24, 9, 14, 12, 19,
-    22, 21, 2, 5, 1, 23, 4, 20, 14, 13, 17, 9, 12, 22, 21, 23, 6, 7, 8, 0, 10, 3, 15, 16, 11, 18, 24, 19, 2, 1,
-    5, 4, 13, 20, 17, 9, 14, 12, 22, 21, 23,
+    1, 3, 2, 5, 1, 3, 6, 7, 5, 9, 8, 4, 7, 12, 11, 10, 9, 13, 8, 4, 14, 12, 10, 14, 17, 16, 12, 0, 13, 18, 10,
+    4, 16, 11, 17, 19, 8, 22, 13, 15, 21, 18, 20, 9, 11, 14, 19, 16, 2, 22, 17, 0, 1, 21, 15, 6, 18, 7, 20, 5,
+    3, 19, 2, 22, 0, 21, 15, 20, 22, 6, 12, 4, 10, 8, 13, 9, 14, 16, 11, 1, 17, 7, 3, 5, 18, 2, 19, 0, 21, 15,
+    20, 6, 22,
 )
 MARKS = (
-    0, 0, 0, 0, 0, 0, 0, 0, 0, 0, 0, 0, 0, 0, 1, 1, 1, 2, 2, 3, 4, 5, 5, 7, 7, 10, 13, 14, 14, 15, 15, 16, 17,
-    17,
+    0, 0, 0, 0, 0, 0, 0, 1, 2, 2, 3, 3, 3, 3, 4, 4, 6, 7, 7, 8, 8, 9, 10, 10, 10, 11, 13, 15, 19, 20, 21, 21,
+    21, 22, 23, 23,
 )
-EARLY = 5
+EARLY = 3
 
 
 def shards(n_dp, *args):
@@ -650,7 +655,7 @@
         outputs.append(("rows", sds((block, columns), F32), any_spec))
     else:
         outputs.append(("grads", sds((blocks, block, columns), BF), any_spec))
-    outputs.append(("sums", sds((16, width), F32), vmem))
+    outputs.append(("sums", sds((16, width), F32), any_spec))
     v = pltpu.VMEM
     dma = pltpu.SemaphoreType.DMA
     scratch = [
@@ -705,13 +710,13 @@
         ("g_db", sds((block,), F32), vmem), ("g_gain2", sds((block,), F32), vmem), ("g_shift2", sds((block,), F32), vmem),
     ]
     sources = ("os", "ol", "dxs", "dxl", "rows", "sums")
-    names = ["in_" + n for n in sources] + [f[0] for f in finals] + ["held_" + n for n in sources[:5]] + ["into", "out"]
+    names = ["in_" + n for n in sources] + [f[0] for f in finals] + ["held_" + n for n in sources] + ["into", "out"]
     results = pl.pallas_call(
         functools.partial(place_results, n_dp, names),
         out_shape=[f[1] for f in finals],
-        in_specs=[any_spec] * 5 + [vmem],
+        in_specs=[any_spec] * 6,
         out_specs=[f[2] for f in finals],
-        scratch_shapes=[v(got[n].shape, got[n].dtype) for n in sources[:5]] + [dma((10,)), dma((10,))],
+        scratch_shapes=[v(got[n].shape, got[n].dtype) for n in sources] + [dma((11,)), dma((10,))],
         cost_estimate=pl.CostEstimate(flops=0, bytes_accessed=8 << 20, transcendentals=0),
         compiler_params=pltpu.CompilerParams(vmem_limit_bytes=62 << 20),
     )(*[got[n] for n in sources])
@@ -731,17 +736,26 @@
     moves += [(getattr(r, "in_" + n), getattr(r, "held_" + n), getattr(r, n)) for n in ("os", "ol", "dxs", "dxl")]
     into = [pltpu.make_async_copy(source, held, r.into.at[j]) for j, (source, held, _) in enumerate(moves)]
     out = [pltpu.make_async_copy(held, target, r.out.at[j]) for j, (_, held, target) in enumerate(moves)]
+    vectors = pltpu.make_async_copy(r.in_sums, r.held_sums, r.into.at[10])
+    vectors.start()
     for cp in into:
         cp.start()
+    vectors.wait()
+    vector_results(r)
     for cp, back in zip(into, out):
         cp.wait()
         back.start()
+    for cp in out:
+        cp.wait()
+
+
+def vector_results(r):
     dp = lax.axis_index("dp")
     local = r.gq.shape[1]
-    width = r.in_sums.shape[1]
+    width = r.held_sums.shape[1]
 
     def turn(start):
-        return pltpu.roll(r.in_sums[...], lax.rem(2 * width - start, width), 1)
+        return pltpu.roll(r.held_sums[...], lax.rem(2 * width - start, width), 1)
 
     size = r.g_ob.shape[0]
     turned = turn(dp * size)
@@ -754,8 +768,6 @@
     size = r.g_ub.shape[0]
     turned = turn(lax.rem(dp * size, width))
     r.g_ub[...] = jnp.where(dp * size < width, turned[1:2, :size], turned[2:3, :size]).reshape(size)
-    for cp in out:
-        cp.wait()
 
 
 def solution(mesh):

time: 94.4 us -> 92.4 us (0.979)
  Pallas kernels: 92.7 us -> 90.7 us
    pallas_call x1, Pallas kernels: 87.6 us -> 86.4 us  [shards(): pl.pallas_call(functools.partial(layer, reduce_here, names), out_shape=[o...]
where the time goes in v1:
time: 92.4 us; the launch traced here: 92.2 us
  Pallas kernels  90.7 us (98%)
  between operations  1.5 us (2%)
    pallas_call x1, Pallas kernels, shards(): pl.pallas_call(functools.partial(layer, reduce_here, names), out_shape=[o...  86.4 us
    pallas_call x1, Pallas kernels, shards(): pl.pallas_call(functools.partial(place_results, n_dp, names), out_shape=[...  4.33 us

profile of v1, /device:TPU:0, one launch (start us, length us, event | category | flops | bytes accessed | tf_op | source)
XLA Modules:
  0.0 92.2 jit_solution(6795115056936805827)
XLA Ops:
  1.3 86.4 %shard_map.357 = (bf16[4,128,768]{2,1,0:T(8,128)(2,1)}, bf16[1,512,768]{2,1,0:T(8,128)(2,1)}, bf16[4,128,768]{2,1,0:T(8,128)(2,1)}, bf16[1,512,768]{2,1,0:T(8,12...) custom-call(s32[4]{0:T(128)} %refs_0_.1, s32[1]{0:T(128)S(6)} %copy.41.refs_1_, s32[1,2]{1,0:T(1,128)} %refs_2_.1, ...), custom_call_target="tpu_custom_call" | custom-call | flops 19327352832 | bytes 20971520 | tf_op jit(solution)/shard_map/pallas_call | solution.py:684
  87.7 4.3 %shard_map.358 = (bf16[4,128,768]{2,1,0:T(8,128)(2,1)}, bf16[1,512,768]{2,1,0:T(8,128)(2,1)}, bf16[4,128,768]{2,1,0:T(8,128)(2,1)}, bf16[1,512,768]{2,1,0:T(8,12...) custom-call(bf16[4,128,768]{2,1,0:T(8,128)(2,1)} %get-tuple-element., ...), custom_call_target="tpu_custom_call" | custom-call | bytes 8388608 | tf_op jit(solution)/shard_map/pallas_call | solution.py:714

commit v2 on v1

--- a/solution.py
+++ b/solution.py
@@ -727,13 +727,12 @@
     r = Refs()
     for name, ref in zip(names, refs, strict=True):
         setattr(r, name, ref)
-    moves = []
+    moves = [(getattr(r, "in_" + n), getattr(r, "held_" + n), getattr(r, n)) for n in ("os", "ol", "dxs", "dxl")]
     at = 0
     for ref in (r.gdown, r.gup, r.gout, r.gq, r.gk, r.gv):
         cols = slice(at, at + ref.shape[1])
         moves.append((r.in_rows.at[:, cols], r.held_rows.at[:, cols], ref))
         at += ref.shape[1]
-    moves += [(getattr(r, "in_" + n), getattr(r, "held_" + n), getattr(r, n)) for n in ("os", "ol", "dxs", "dxl")]
     into = [pltpu.make_async_copy(source, held, r.into.at[j]) for j, (source, held, _) in enumerate(moves)]
     out = [pltpu.make_async_copy(held, target, r.out.at[j]) for j, (_, held, target) in enumerate(moves)]
     vectors = pltpu.make_async_copy(r.in_sums, r.held_sums, r.into.at[10])

time: 92.4 us -> 92 us (level)
  no operation moved by 1% of the time
where the time goes in v2:
time: 92 us; the launch traced here: 91.8 us
  Pallas kernels  90.3 us (98%)
  between operations  1.5 us (2%)
    pallas_call x1, Pallas kernels, shards(): pl.pallas_call(functools.partial(layer, reduce_here, names), out_shape=[o...  86.4 us
    pallas_call x1, Pallas kernels, shards(): pl.pallas_call(functools.partial(place_results, n_dp, names), out_shape=[...  3.84 us

profile of v2, /device:TPU:0, one launch (start us, length us, event | category | flops | bytes accessed | tf_op | source)
XLA Modules:
  0.0 91.8 jit_solution(2848623141695556073)
XLA Ops:
  1.3 86.4 %shard_map.357 = (bf16[4,128,768]{2,1,0:T(8,128)(2,1)}, bf16[1,512,768]{2,1,0:T(8,128)(2,1)}, bf16[4,128,768]{2,1,0:T(8,128)(2,1)}, bf16[1,512,768]{2,1,0:T(8,12...) custom-call(s32[4]{0:T(128)} %refs_0_.1, s32[1]{0:T(128)S(6)} %copy.41.refs_1_, s32[1,2]{1,0:T(1,128)} %refs_2_.1, ...), custom_call_target="tpu_custom_call" | custom-call | flops 19327352832 | bytes 20971520 | tf_op jit(solution)/shard_map/pallas_call | solution.py:684
  87.7 3.8 %shard_map.358 = (bf16[4,128,768]{2,1,0:T(8,128)(2,1)}, bf16[1,512,768]{2,1,0:T(8,128)(2,1)}, bf16[4,128,768]{2,1,0:T(8,128)(2,1)}, bf16[1,512,768]{2,1,0:T(8,12...) custom-call(bf16[4,128,768]{2,1,0:T(8,128)(2,1)} %get-tuple-element., ...), custom_call_target="tpu_custom_call" | custom-call | bytes 8388608 | tf_op jit(solution)/shard_map/pallas_call | solution.py:714
